TPU v7x, 32 devices: a whole 2x2x4 slice. The times are simulated.
32 devices in a mesh: lat: 8 (over z, x), lev: 4 (over y, core).
Axes of the slice: x: 2, y: 2, z: 4, core: 2. Of those that a mesh axis runs over, the one named last changes fastest.
Arguments:
- particle_mass_fraction: float32 [20, 64, 8, 360], P(None, 'lat', 'lev'), may hold values from 0.1 to 2
- meridional_cfl_factor: float32 [64, 8, 360], P('lat', 'lev'), may hold values from -0.45 to 0.45
- thermal_state_kelvins: float32 [64, 8, 360], P('lat', 'lev'), may hold values from 200 to 300
- logarithmic_barometric_span: float32 [8], P('lev'), may hold values from 0.06 to 0.2
- gravitational_fall_kilometres: float32 [20], replicated, may hold values from 0.02 to 20
- zonal_cfl_factor: float32 [64, 8, 360], P('lat', None, 'lev'), may hold values from -0.45 to 0.45
- collision_rate_matrix: float32 [20, 20], replicated, may hold values from 0.02 to 0.2
Outputs:
- dust_out: float32 [20, 64, 8, 360], P(None, 'lat', None, 'lev')
- height: float32 [64, 8, 360], P('lat', 'lev')
All inputs are finite; a program needn't handle non-finite values.
Results may differ from a plain program's by a relative error of at most 0.000067.
Values sent between devices are 32-bit elements; how exact they have to be, the bound alone decides.
A program may use at most 128 MiB of HBM per device.

v0:
```python
import jax
import jax.numpy as jnp
from jax import lax
from jax.sharding import PartitionSpec as P

specific_air_factor = 0.0293
scale_height = 7.0


def extended_2(x, sides, width, wrap):
    for axis, dim in sides:
        peers, length = (lax.axis_size(axis), x.shape[dim])
        up = [(i, (i + 1) % peers) for i in range(peers if wrap else peers - 1)]
        down = [(j, i) for i, j in up]
        last = lax.slice_in_dim(x, length - width, length, axis=dim)
        leading = lax.slice_in_dim(x, 0, width, axis=dim)
        before = lax.ppermute(last, axis, up)
        after = lax.ppermute(leading, axis, down)
        x = jnp.concatenate([before, x, after], axis=dim)
    return x


def prefix(value, axis, join, neutral):
    count, mine = (lax.axis_size(axis), lax.axis_index(axis))
    pieces = lax.all_gather(value, axis)
    pieces = pieces[::-1]
    mine = count - 1 - mine
    subtotal = jnp.full_like(value, 0) + jnp.asarray(neutral, value.dtype)

    def step(position, subtotal):
        longer = join(subtotal, pieces[position])
        return jnp.where(position < mine, longer, subtotal)

    return lax.fori_loop(0, count - 1, step, subtotal)


def settle_sweep(mixing, settle_rate, inflow):

    def stepper(flux_in, inputs):
        level_mix, level_rate = inputs
        summed = level_mix + flux_in
        return (level_rate / (1.0 + level_rate) * summed, summed / (1.0 + level_rate))

    _, swept = lax.scan(
        stepper, inflow, (jnp.moveaxis(mixing, 2, 0), jnp.moveaxis(settle_rate, 2, 0))
    )
    return jnp.moveaxis(swept, 0, 2)


def add_terms(earlier, later):
    return earlier + later


def on_device(
    particle_mass_fraction,
    meridional_cfl_factor,
    thermal_state_kelvins,
    logarithmic_barometric_span,
    gravitational_fall_kilometres,
    zonal_cfl_factor,
    collision_rate_matrix,
):
    bin_count = particle_mass_fraction.shape[0]
    stacked = jnp.concatenate([particle_mass_fraction, meridional_cfl_factor[None]], 0)
    padded = extended_2(stacked, (("lat", 1),), 1, False)
    rows_below = padded[:bin_count, :-2]
    rows_above = padded[:bin_count, 2:]
    courant_above = padded[bin_count, 2:]
    south_flux = (
        jnp.maximum(meridional_cfl_factor, 0.0) * rows_below
        + jnp.minimum(meridional_cfl_factor, 0.0) * particle_mass_fraction
    )
    north_flux = (
        jnp.maximum(courant_above, 0.0) * particle_mass_fraction
        + jnp.minimum(courant_above, 0.0) * rows_above
    )
    advected = particle_mass_fraction + south_flux - north_flux
    vertical_span_height = (
        specific_air_factor * thermal_state_kelvins * logarithmic_barometric_span[None, :, None]
    )
    column_total = jnp.sum(vertical_span_height, axis=1)
    incoming = prefix(column_total, "lev", add_terms, jnp.zeros_like(column_total))
    height = (
        incoming[:, None, :]
        + jnp.cumsum(vertical_span_height[:, ::-1], axis=1)[:, ::-1]
        - 0.5 * vertical_span_height
    )
    density = jnp.exp(-height / scale_height)
    packed = jnp.concatenate([advected, vertical_span_height[None], density[None]], 0)
    columns = lax.all_to_all(packed, "lev", split_axis=3, concat_axis=2, tiled=True)
    col_thick = columns[bin_count]
    col_density = columns[bin_count + 1]
    settle_rate = gravitational_fall_kilometres[:, None, None, None] / col_thick[None]
    inflow = jnp.zeros((bin_count, columns.shape[1], columns.shape[3]), jnp.float32)
    settled = settle_sweep(columns[:bin_count], settle_rate, inflow)
    extended = extended_2(
        jnp.concatenate([settled, zonal_cfl_factor[None]], 0), (("lev", 3),), 1, True
    )
    west_mix = extended[:bin_count, :, :, :-2]
    east_mix = extended[:bin_count, :, :, 2:]
    courant_east = extended[bin_count, :, :, 2:]
    west_flux = (
        jnp.maximum(zonal_cfl_factor, 0.0) * west_mix + jnp.minimum(zonal_cfl_factor, 0.0) * settled
    )
    east_flux = jnp.maximum(courant_east, 0.0) * settled + jnp.minimum(courant_east, 0.0) * east_mix
    moved = settled + west_flux - east_flux
    merging = jnp.tril(collision_rate_matrix, -1) - jnp.triu(collision_rate_matrix, 1)
    coag_rate = jnp.einsum("bc,clkx->blkx", merging, moved, precision=lax.Precision.HIGHEST)
    return (moved + col_density * moved * coag_rate, height)


def solution(mesh):
    in_specs = (
        P(None, "lat", "lev", None),
        P("lat", "lev", None),
        P("lat", "lev", None),
        P("lev"),
        P(),
        P("lat", None, "lev"),
        P(),
    )
    out_specs = (P(None, "lat", None, "lev"), P("lat", "lev", None))
    return jax.shard_map(
        on_device, mesh=mesh, in_specs=in_specs, out_specs=out_specs, check_vma=False
    )
```

profile of v0, /device:TPU:0, one launch (start us, length us, event | category | flops | bytes accessed | tf_op | source)
XLA Modules:
  0.0 57.4 jit_solution(17528665692314259171)
XLA Ops:
  0.6 0.0 copy-start
  0.6 1.0 %pad_maximum_fusion.11 = (f32[21,1,2,360]{3,2,1,0:T(2,128)S(1)}, f32[21,1,2,360]{3,2,1,0:T(2,128)S(1)}) fusion(f32[1,8,2,360]{3,2,1,0:T(2,128)} %bitcast.67, f32[20,8,2,360]{3,2,1,0:T(2,128)} %param.11), kind=kLoop, calls=%fused_computation.41 | loop fusion | flops 30240 | bytes 604800 | tf_op jit(solution)/shard_map/slice | solution.py:15
  1.7 1.3 %collective-permute-start.1 = (f32[21,1,2,360]{3,2,1,0:T(2,128)S(1)}, f32[21,1,2,360]{3,2,1,0:T(2,128)S(1)}, u32[]{:S(2)}, u32[]{:S(2)}) collective-permute-start(f32[21,1,2,360]{3,2,1,0:T(2,128)S(1)} %get-tuple-element.233), channel_id=1, source_target_pairs={{4,0},{8,4},{12,8},{16,12},{20,16},{24,20},{28,24},{5,1},{9,5},{13... | collective-permute-start | bytes 181448 | tf_op jit(solution)/shard_map/ppermute | solution.py:18
  3.0 5.5 %collective-permute-start = (f32[21,1,2,360]{3,2,1,0:T(2,128)S(1)}, f32[21,1,2,360]{3,2,1,0:T(2,128)S(1)}, u32[]{:S(2)}, u32[]{:S(2)}) collective-permute-start(f32[21,1,2,360]{3,2,1,0:T(2,128)S(1)} %get-tuple-element.232), channel_id=1, source_target_pairs={{0,4},{4,8},{8,12},{12,16},{16,20},{20,24},{24,28},{1,5},{5,9},{9,... | collective-permute-start | bytes 181448 | tf_op jit(solution)/shard_map/ppermute | solution.py:17
  8.4 0.8 %broadcast_maximum_fusion.2 = (f32[8,2,360]{2,1,0:T(2,128)S(1)}, f32[8,2,360]{2,1,0:T(2,128)S(1)}) fusion(f32[8,2,360]{2,1,0:T(2,128)} %param.12), kind=kLoop, calls=%fused_computation.60 | loop fusion | flops 11520 | bytes 69120 | tf_op jit(solution)/shard_map/max | solution.py:70
  9.2 0.7 %broadcast_multiply_fusion = f32[2]{0:T(128)S(1)} fusion(f32[2]{0:T(128)} %param.14), kind=kLoop, calls=%fused_computation.64 | loop fusion | flops 2 | bytes 16 | tf_op jit(solution)/shard_map/mul | solution.py:79
  9.9 0.8 %fusion.29 = (f32[8,360]{1,0:T(8,128)S(1)}, f32[8,2,360]{2,0,1:T(8,128)S(1)}) fusion(f32[2]{0:T(128)S(1)} %broadcast_multiply_fusion, f32[8,2,360]{2,1,0:T(2,128)} %param.13), kind=kLoop, calls=%fused_computation.67 | loop fusion | flops 8640 | bytes 57608 | tf_op jit(solution)/shard_map/reduce_sum | solution.py:81
  10.7 0.1 fusion.31
  10.8 5.3 %all-gather = f32[32,360]{1,0:T(8,128)S(1)} all-gather(f32[8,360]{1,0:T(8,128)S(1)} %get-tuple-element.224), channel_id=2, replica_groups=mesh['lat'=8,'lev'=4] {'lev'}, dimensions={0}, use_global_device_ids=true | all-gather | bytes 57600 | tf_op jit(solution)/shard_map/all_gather | solution.py:25
  16.1 0.1 while.27
  16.2 0.6 %exponential_bitcast_fusion = (f32[1,8,2,360]{3,1,2,0:T(8,128)S(1)}, f32[8,2,360]{2,0,1:T(8,128)}) fusion(f32[8,2,360]{2,0,1:T(8,128)S(1)} %get-tuple-element.225, f32[8,2,360]{2,0,1:T(8,128)S(1)} %fusion.31, f32[8,360]{1,0:T(8,128)S(1)} %get-tuple-element.108), kind=kLoop, calls=%fused_computation.45 | loop fusion | flops 28800 | bytes 103680 | tf_op jit(solution)/shard_map/broadcast_in_dim | solution.py:89
  16.8 0.0 collective-permute-done.1
  16.8 0.8 %maximum_bitcast_fusion = (f32[8,2,360]{2,1,0:T(2,128)S(1)}, f32[1,8,2,360]{3,2,1,0:T(2,128)S(1)}) fusion(f32[21,1,2,360]{3,2,1,0:T(2,128)S(1)} %collective-permute-done.1, f32[1,8,2,360]{3,2,1,0:T(2,128)} %bitcast.68, f32[20,8,2,360]{3,2,1,0:T(2,128)} %param.11), kind=kLoop, calls=%fused_computation.48 | loop fusion | flops 17280 | bytes 590400 | tf_op jit(solution)/shard_map/mul | solution.py:74
  17.7 0.0 collective-permute-done
  17.7 1.7 %pad_maximum_fusion.8 = (f32[20,8,2,360]{3,2,1,0:T(2,128)S(1)}, f32[20,8,2,360]{3,2,1,0:T(2,128)S(1)}) fusion(f32[21,1,2,360]{3,2,1,0:T(2,128)S(1)} %collective-permute-done, f32[1,8,2,360]{3,2,1,0:T(2,128)} %bitcast.69, f32[20,8,2,360]{3,2,1,0:T(2,128)} %param.11, f32[21,1,2,360]{3,2,1,0:T(2,128)S(1)} %collective-permute-done.1), kind=kLoop, calls=%fused_computation.27 | loop fusion | flops 460800 | bytes 1526400 | tf_op jit(solution)/shard_map/concatenate | solution.py:19
  19.4 0.1 fusion.14
  19.6 1.3 %copy.255 = f32[22,8,2,360]{0,1,2,3:T(8,128)S(1)} copy(f32[22,8,2,360]{3,1,2,0:T(8,128)S(1)} %pad_maximum_fusion.5) | data formatting | bytes 1013760 | tf_op jit(solution)/shard_map/concatenate | solution.py:89
  20.9 0.0 copy-start.2
  20.9 3.7 %reshape.18 = f32[4,1,31680]{2,1,0:T(1,128)} reshape(f32[360,2,8,22]{3,2,1,0:T(8,128)S(1)} %bitcast.60) | data formatting | bytes 1013760
  24.6 3.5 %all-to-all-start = ((f32[4,1,31680]{2,1,0:T(1,128)}), f32[4,1,31680]{2,1,0:T(1,128)S(1)}, u32[]{:S(2)}, u32[]{:S(2)}) async-start(f32[4,1,31680]{2,1,0:T(1,128)} %reshape.18), calls=%async_computation | async-start | bytes 1015808 | tf_op jit(solution)/shard_map/all_to_all | solution.py:90
  28.1 0.6 %broadcast_maximum_fusion.1 = (f32[8,8,90]{2,1,0:T(8,128)}, f32[8,8,90]{2,1,0:T(8,128)}) fusion(f32[8,8,90]{2,1,0:T(8,128)S(1)} %copy-done.2), kind=kLoop, calls=%fused_computation.52 | loop fusion | flops 11520 | bytes 69120 | tf_op jit(solution)/shard_map/max | solution.py:103
  28.7 8.1 %all-to-all-done = f32[4,1,31680]{2,1,0:T(1,128)S(1)} async-done(((f32[4,1,31680]{2,1,0:T(1,128)}), f32[4,1,31680]{2,1,0:T(1,128)S(1)}, u32[]{:S(2)}, u32[]{:S(2)}) %all-to-all-start) | async-done | bytes 506912 | tf_op jit(solution)/shard_map/all_to_all | solution.py:90
  36.8 0.6 %broadcast.65 = f32[]{:T(128)} broadcast(f32[]{:T(128)} %constant.131), dimensions={} | broadcast | bytes 8 | tf_op jit(solution)/shard_map/all_to_all | solution.py:90
  37.4 2.2 %reduce = f32[4,31680]{1,0:T(4,128)S(1)} reduce(f32[4,1,31680]{2,1,0:T(1,128)S(1)} %all-to-all-done, f32[]{:T(128)} %broadcast.65), dimensions={1}, to_apply=%all_to_all.11.reduce_sub_computation | reduce | bytes 1013764 | tf_op jit(solution)/shard_map/all_to_all | solution.py:90
  39.6 3.5 %reshape.19 = f32[360,2,8,22]{3,2,1,0:T(8,128)S(1)} reshape(f32[4,31680]{1,0:T(4,128)S(1)} %reduce) | data formatting | bytes 1013760
  43.1 0.0 copy-start.7
  43.1 2.2 %copy.270 = f32[22,8,2,4,90]{4,3,1,2,0:T(4,128)} copy(f32[22,8,2,4,90]{0,1,2,4,3:T(8,128)S(1)} %bitcast.59) | data formatting | bytes 1013760 | tf_op jit(solution)/shard_map/all_to_all | solution.py:90
  45.3 0.8 %fusion.30 = (f32[1,8,4,2,90]{4,2,1,3,0:T(4,128)S(1)}, f32[1,8,4,2,90]{4,2,1,3,0:T(4,128)S(1)}) fusion(f32[22,8,4,2,90]{4,2,1,3,0:T(4,128)} %bitcast.65), kind=kLoop, calls=%fused_computation.68 | loop fusion | bytes 92160 | tf_op jit(solution)/shard_map/slice | solution.py:92
  46.1 1.1 %slice.65 = f32[20,8,4,2,90]{4,2,1,3,0:T(4,128)S(1)} slice(f32[22,8,4,2,90]{4,2,1,3,0:T(4,128)} %bitcast.66), slice={[0:20], [0:8], [0:4], [0:2], [0:90]} | slice | bytes 921600 | tf_op jit(solution)/shard_map/slice | solution.py:95
  47.3 0.0 copy-start.3
  47.4 0.1 broadcast_divide_fusion
  47.5 0.8 %while.28 = (s32[]{:T(128)}, f32[20,8,90]{2,1,0:T(8,128)S(1)}, f32[8,20,8,90]{3,2,1,0:T(8,128)S(1)}, f32[8,20,8,90]{3,2,1,0:T(8,128)S(1)}, f32[8,20,8,90]{3,2,1,0:T(8,128)S(1)}, /*index=5*/s32[]{:T(128)}, s32[]{:T(128)}) while((s32[]{:T(128)}, f32[20,8,90]{2,1,0:T(8,128)S(1)}, f32[8,20,8,90]{3,2,1,0:T(8,128)S(1)}, ...), condition=%wide.region_5.6_spmd.clone, body=%wide.region_4.5_spmd.clone.sunk | while | flops 129603 | bytes 558176 | solution.py:44
  48.3 0.0 copy-start.4
  48.3 0.1 copy.291
  48.5 0.4 slice_maximum_fusion
  48.9 0.0 copy-start.8
  48.9 0.5 copy.263
  49.3 0.0 collective-permute-start.3
  49.4 0.6 %copy.268 = f32[8,2,360]{2,1,0:T(2,128)} copy(f32[8,2,360]{2,0,1:T(8,128)S(1)} %copy-done.4) | data formatting | bytes 46080
  50.0 0.5 copy.261
  50.5 0.7 %collective-permute-start.2 = (f32[21,8,8,1]{0,2,3,1:T(8,128)S(1)}, f32[21,8,8,1]{0,2,3,1:T(8,128)S(1)}, u32[]{:S(2)}, u32[]{:S(2)}) collective-permute-start(f32[21,8,8,1]{0,2,3,1:T(8,128)S(1)} %copy.261), channel_id=1, source_target_pairs={{0,1},{1,2},{2,3},{3,0},{4,5},{5,6},{6,7},{7,4},{8,9},{9,10},{10,1... | collective-permute-start | bytes 16136 | tf_op jit(solution)/shard_map/ppermute | solution.py:17
  51.2 0.0 collective-permute-done.3
  51.2 0.5 copy.264
  51.7 0.3 broadcast_maximum_fusion
  52.0 2.0 %collective-permute-done.2 = f32[21,8,8,1]{0,2,3,1:T(8,128)S(1)} collective-permute-done((f32[21,8,8,1]{0,2,3,1:T(8,128)S(1)}, f32[21,8,8,1]{0,2,3,1:T(8,128)S(1)}, u32[]{:S(2)}, u32[]{:S(2)}) %collective-permute-start.2) | collective-permute-done | bytes 5408 | tf_op jit(solution)/shard_map/ppermute | solution.py:17
  54.1 0.5 copy.262
  54.6 1.9 %fusion.3 = f32[20,8,8,90]{3,0,2,1:T(8,128)S(1)} fusion(f32[21,8,8,1]{3,0,2,1:T(8,128)S(1)} %copy.264, f32[1,8,8,90]{3,0,2,1:T(1,128)S(1)} %bitcast.73, f32[20,8,8,90]{3,0,2,1:T(8,128)S(1)} %bitcast.63, f32[21,8,8,1]{3,0,2,1:T(8,128)S(1)} %copy.262, f32[8,8,90]{2,1,0:T(8,128)S(1)} %copy.266, f32[8,8,90]{2,1,0:T(8,128)S(1)} %bitcast.78, ...), kind=kOutput, calls=%fused_computation.8 | convolution fusion | flops 30760400 | bytes 1072272 | tf_op jit(solution)/shard_map/bc,clkx->blkx/dot_general | solution.py:108
  56.5 1.0 %copy.267 = f32[20,8,8,90]{3,2,1,0:T(8,128)} copy(f32[20,8,8,90]{3,0,2,1:T(8,128)S(1)} %fusion.3) | data formatting | bytes 921600
  (48 shorter events, 0.8 us)
Async XLA Ops:
  0.6 18.8 %copy-start = (f32[20,8,2,360]{3,2,1,0:T(2,128)S(1)}, f32[20,8,2,360]{3,2,1,0:T(2,128)}, u32[]{:S(2)}) copy-start(f32[20,8,2,360]{3,2,1,0:T(2,128)} %param.11) | copy-start | bytes 1382404
  1.7 15.2 %collective-permute-start.1 = (f32[21,1,2,360]{3,2,1,0:T(2,128)S(1)}, f32[21,1,2,360]{3,2,1,0:T(2,128)S(1)}, u32[]{:S(2)}, u32[]{:S(2)}) collective-permute-start(f32[21,1,2,360]{3,2,1,0:T(2,128)S(1)} %get-tuple-element.233), channel_id=1, source_target_pairs={{4,0},{8,4},{12,8},{16,12},{20,16},{24,20},{28,24},{5,1},{9,5},{13... | collective-permute-start | bytes 181448 | tf_op jit(solution)/shard_map/ppermute | solution.py:18
  3.0 14.7 %collective-permute-start = (f32[21,1,2,360]{3,2,1,0:T(2,128)S(1)}, f32[21,1,2,360]{3,2,1,0:T(2,128)S(1)}, u32[]{:S(2)}, u32[]{:S(2)}) collective-permute-start(f32[21,1,2,360]{3,2,1,0:T(2,128)S(1)} %get-tuple-element.232), channel_id=1, source_target_pairs={{0,4},{4,8},{8,12},{12,16},{16,20},{20,24},{24,28},{1,5},{5,9},{9,... | collective-permute-start | bytes 181448 | tf_op jit(solution)/shard_map/ppermute | solution.py:17
  20.9 7.2 %copy-start.2 = (f32[8,8,90]{2,1,0:T(8,128)S(1)}, f32[8,8,90]{2,1,0:T(8,128)}, u32[]{:S(2)}) copy-start(f32[8,8,90]{2,1,0:T(8,128)} %param.16) | copy-start | bytes 69124
  24.6 12.3 %all-to-all-start = ((f32[4,1,31680]{2,1,0:T(1,128)}), f32[4,1,31680]{2,1,0:T(1,128)S(1)}, u32[]{:S(2)}, u32[]{:S(2)}) async-start(f32[4,1,31680]{2,1,0:T(1,128)} %reshape.18), calls=%async_computation | async-start | bytes 1015808 | tf_op jit(solution)/shard_map/all_to_all | solution.py:90
  43.1 4.3 %copy-start.7 = (f32[20]{0:T(128)S(1)}, f32[20]{0:T(128)}, u32[]{:S(2)}) copy-start(f32[20]{0:T(128)} %param.15) | copy-start | bytes 244
  45.3 2.2 %copy-start.1 = (f32[8,20,8,90]{3,2,1,0:T(8,128)S(1)}, f32[8,20,8,90]{3,2,1,0:T(8,128)}, u32[]{:S(2)}) copy-start(f32[8,20,8,90]{3,2,1,0:T(8,128)} %custom-call.2) | copy-start | bytes 1382404
  47.3 1.1 %copy-start.3 = (f32[8,8,90]{2,1,0:T(8,128)S(1)}, f32[8,8,90]{2,1,0:T(8,128)}, u32[]{:S(2)}) copy-start(f32[8,8,90]{2,1,0:T(8,128)} %param.16) | copy-start | bytes 69124
  48.3 1.1 %copy-start.4 = (f32[8,2,360]{2,0,1:T(8,128)S(1)}, f32[8,2,360]{2,0,1:T(8,128)}, u32[]{:S(2)}) copy-start(f32[8,2,360]{2,0,1:T(8,128)} %get-tuple-element.223) | copy-start | bytes 69124
  48.8 5.7 %copy-start.5 = (f32[8,8,90]{2,1,0:T(8,128)S(1)}, f32[8,8,90]{2,1,0:T(8,128)}, u32[]{:S(2)}) copy-start(f32[8,8,90]{2,1,0:T(8,128)} %get-tuple-element.234) | copy-start | bytes 69124
  48.8 5.7 %copy-start.6 = (f32[8,8,90]{2,1,0:T(8,128)S(1)}, f32[8,8,90]{2,1,0:T(8,128)}, u32[]{:S(2)}) copy-start(f32[8,8,90]{2,1,0:T(8,128)} %get-tuple-element.235) | copy-start | bytes 69124
  48.9 5.7 %copy-start.8 = (f32[20,20]{1,0:T(8,128)S(1)}, f32[20,20]{1,0:T(8,128)}, u32[]{:S(2)}) copy-start(f32[20,20]{1,0:T(8,128)} %param.17) | copy-start | bytes 4804
  49.3 1.9 %collective-permute-start.3 = (f32[21,8,8,1]{0,2,3,1:T(8,128)S(1)}, f32[21,8,8,1]{0,2,3,1:T(8,128)S(1)}, u32[]{:S(2)}, u32[]{:S(2)}) collective-permute-start(f32[21,8,8,1]{0,2,3,1:T(8,128)S(1)} %copy.263), channel_id=1, source_target_pairs={{1,0},{2,1},{3,2},{0,3},{5,4},{6,5},{7,6},{4,7},{9,8},{10,9},{11,1... | collective-permute-start | bytes 16136 | tf_op jit(solution)/shard_map/ppermute | solution.py:18
  50.5 3.5 %collective-permute-start.2 = (f32[21,8,8,1]{0,2,3,1:T(8,128)S(1)}, f32[21,8,8,1]{0,2,3,1:T(8,128)S(1)}, u32[]{:S(2)}, u32[]{:S(2)}) collective-permute-start(f32[21,8,8,1]{0,2,3,1:T(8,128)S(1)} %copy.261), channel_id=1, source_target_pairs={{0,1},{1,2},{2,3},{3,0},{4,5},{5,6},{6,7},{7,4},{8,9},{9,10},{10,1... | collective-permute-start | bytes 16136 | tf_op jit(solution)/shard_map/ppermute | solution.py:17
where the time goes:
time: 57.9 us; the launch traced here: 57.4 us
  local copies, waits for them, and re-layouts  17 us (29%)
  starting transfers between devices  11 us (19%)
  other arithmetic  10.8 us (19%)
  waiting for transfers between devices  10.1 us (17%)
  blocking collectives  5.29 us (9%)
  matrix products  1.89 us (3%)
  between operations  1.01 us (2%)
    unnamed x22, local copies, waits for them, and re-layouts  8.74 us
    all_to_all x1, waiting for transfers between devices, on_device(): lax.all_to_all(packed, 'lev', split_axis=3, concat_axis=2, tiled=True)  8.13 us
    ppermute x2, starting transfers between devices, extended_2(): before = lax.ppermute(last, axis, up)  6.16 us
    all_gather x1, blocking collectives, prefix(): pieces = lax.all_gather(value, axis)  5.29 us
    all_to_all x1, starting transfers between devices, on_device(): lax.all_to_all(packed, 'lev', split_axis=3, concat_axis=2, tiled=True)  3.47 us
    all_to_all x2, local copies, waits for them, and re-layouts, on_device(): lax.all_to_all(packed, 'lev', split_axis=3, concat_axis=2, tiled=True)  2.8 us
    all_to_all x1, other arithmetic, on_device(): lax.all_to_all(packed, 'lev', split_axis=3, concat_axis=2, tiled=True)  2.16 us
    ppermute x2, waiting for transfers between devices, extended_2(): before = lax.ppermute(last, axis, up)  2.01 us
  transfers between devices with their start and end apart: 5, of which 2 were waited for; matrix products, arithmetic and copies ran while one was open for 11% of the time, Pallas kernels for 0%

commit v1 on v0

v1 whole, which is shorter than its diff:
```python
import functools

import jax
import jax.numpy as jnp
from jax import lax
from jax.experimental import pallas as pl
from jax.experimental.pallas import tpu as pltpu
from jax.sharding import PartitionSpec as P

specific_air_factor = 0.0293
scale_height = 7.0
LANES = 128
MESH = pl.DeviceIdType.MESH
HIGHEST = lax.Precision.HIGHEST


def widen(x):
    short = -x.shape[-1] % LANES
    if short:
        x = jnp.concatenate([x, jnp.zeros((*x.shape[:-1], short), x.dtype)], -1)
    return x


def lon_block(tile, total, width, block):
    axis = 2
    count = -(-total // LANES)
    last = total % LANES
    start = block * width - 1
    c, off = start // LANES, start % LANES

    def piece(i):
        if i < 0:
            return pltpu.roll(tile(count - 1), (LANES - last) % LANES, axis)
        if i == count:
            return tile(0)
        x = tile(i)
        if i == count - 1 and last and total < start + width + 2:
            lane = lax.broadcasted_iota(jnp.int32, x.shape, axis)
            x = jnp.where(lane < last, x, pltpu.roll(tile(0), last, axis))
        return x

    x = piece(c)
    if off + width + 2 > LANES:
        lane = lax.broadcasted_iota(jnp.int32, x.shape, axis)
        x = jnp.where(lane >= off, x, piece(c + 1))
    return pltpu.roll(x, (2 * LANES - off - 1) % LANES, axis)


def kernel(
    n_lat, n_lev,
    q_ref, mc_ref, temp_ref, span_ref, fall_ref, zc_ref, rate_ref,
    out_ref, height_ref,
    main_s, main_r, thick_s, thick_r, north_s, north_r, south_s, south_r,
    tot_s, tot_r, zc_s, zc_r, fall_v, kron, dens,
    main_ss, main_rs, thick_ss, thick_rs, north_ss, north_rs, south_ss, south_rs,
    tot_ss, tot_rs, zc_sem, own_sem,
):
    i, j = lax.axis_index("lat"), lax.axis_index("lev")
    bins, rows, levels, total = q_ref.shape
    width = total // n_lev
    left, right = lax.rem(j + n_lev - 1, n_lev), lax.rem(j + 1, n_lev)
    has_south, has_north = i > 0, i < n_lat - 1

    barrier = pltpu.get_barrier_semaphore()
    for d in range(1, n_lev):
        pl.semaphore_signal(barrier, inc=1, device_id=(i, lax.rem(j + d, n_lev)), device_id_type=MESH)

    @pl.when(has_south)
    def _():
        for m in range(n_lev):
            pl.semaphore_signal(barrier, inc=1, device_id=(i - 1, m), device_id_type=MESH)

    @pl.when(has_north)
    def _():
        for m in range(n_lev):
            pl.semaphore_signal(barrier, inc=1, device_id=(i + 1, m), device_id_type=MESH)

    thick = [specific_air_factor * temp_ref[:, k, :] * span_ref[k] for k in range(levels)]
    tot = thick[0]
    for k in range(1, levels):
        tot = tot + thick[k]
    tot_s[...] = widen(tot)
    for m in range(n_lev):
        for k in range(levels):
            wide = widen(thick[k])[None]
            tile = lambda c: wide[:, :, c * LANES : (c + 1) * LANES]
            thick_s[m, k] = lon_block(tile, total, width, m)[0]
    zc_s[...] = widen(zc_ref[...])

    peers = n_lev - 1 + n_lev * (jnp.minimum(i, 1) + jnp.minimum(n_lat - 1 - i, 1))
    pl.semaphore_wait(barrier, peers)

    def thick_copy(m):
        return pltpu.make_async_remote_copy(
            thick_s.at[m], thick_r.at[j], thick_ss.at[m], thick_rs.at[j], (i, m), MESH)

    def main_copy(m):
        return pltpu.make_async_remote_copy(
            main_s.at[m], main_r.at[j], main_ss.at[m], main_rs.at[j], (i, m), MESH)

    def tot_copy(m):
        return pltpu.make_async_remote_copy(
            tot_s, tot_r.at[j], tot_ss.at[m], tot_rs.at[j], (i, m), MESH)

    def north_copy(m):
        return pltpu.make_async_remote_copy(
            north_s.at[m], north_r.at[j], north_ss.at[m], north_rs.at[j], (i + 1, m), MESH)

    def south_copy(m):
        return pltpu.make_async_remote_copy(
            south_s.at[m], south_r.at[j], south_ss.at[m], south_rs.at[j], (i - 1, m), MESH)

    zc_copy = pltpu.make_async_remote_copy(
        zc_s, zc_r, zc_sem.at[0], zc_sem.at[1], (i, left), MESH)

    for m in range(n_lev):
        @pl.when(j != m)
        def _():
            thick_copy(m).start()
    zc_copy.start()

    last = total - (total // LANES) * LANES

    def tile_of(ref, k):
        def tile(c):
            stop = min((c + 1) * LANES, total)
            return widen(ref[:, :, k, c * LANES : stop])
        return tile

    def mc_tile(k):
        def tile(c):
            stop = min((c + 1) * LANES, total)
            return widen(mc_ref[:, k, c * LANES : stop])[None]
        return tile

    for m in range(n_lev):
        for k in range(levels):
            main_s[m, k, pl.ds(0, bins)] = lon_block(tile_of(q_ref, k), total, width, m)
            main_s[m, k, pl.ds(bins, 1)] = lon_block(mc_tile(k), total, width, m)

        @pl.when(j != m)
        def _():
            main_copy(m).start()

        for k in range(levels):
            south_s[m, k, pl.ds(0, bins + 1)] = main_s[m, k, :, 0, :]
            north_s[m, k, pl.ds(0, bins + 1)] = main_s[m, k, :, rows - 1, :]
        pad = south_s.shape[2] - bins - 1
        if pad:
            zero = jnp.zeros((levels, pad, LANES), jnp.float32)
            south_s[m, :, pl.ds(bins + 1, pad)] = zero
            north_s[m, :, pl.ds(bins + 1, pad)] = zero

        @pl.when(has_south)
        def _():
            south_copy(m).start()

        @pl.when(has_north)
        def _():
            north_copy(m).start()

    for m in range(n_lev):
        @pl.when(j != m)
        def _():
            tot_copy(m).start()

    own = [pltpu.make_async_copy(main_s.at[j], main_r.at[j], own_sem.at[0]),
           pltpu.make_async_copy(thick_s.at[j], thick_r.at[j], own_sem.at[1])]
    for copy in own:
        copy.start()

    @pl.when(jnp.logical_not(has_south))
    def _():
        north_r[...] = jnp.zeros_like(north_r)

    @pl.when(jnp.logical_not(has_north))
    def _():
        south_r[...] = jnp.zeros_like(south_r)

    for b in range(bins):
        fall_v[b] = jnp.full((rows, LANES), fall_ref[b], jnp.float32)
    rate = rate_ref[...]
    r0 = lax.broadcasted_iota(jnp.int32, rate.shape, 0)
    r1 = lax.broadcasted_iota(jnp.int32, rate.shape, 1)
    merging = jnp.where(r1 < r0, rate, jnp.where(r1 > r0, -rate, 0.0))
    cells = bins * rows
    e0 = lax.broadcasted_iota(jnp.int32, (cells, bins), 0)
    e1 = lax.broadcasted_iota(jnp.int32, (cells, bins), 1)
    spread = jnp.where((e0 >= e1 * rows) & (e0 < (e1 + 1) * rows), 1.0, 0.0)
    half = jnp.dot(spread, merging, precision=HIGHEST, preferred_element_type=jnp.float32)
    full = lax.dot_general(half, spread, (((1,), (1,)), ((), ())), precision=HIGHEST,
                           preferred_element_type=jnp.float32)
    k0 = lax.broadcasted_iota(jnp.int32, full.shape, 0)
    k1 = lax.broadcasted_iota(jnp.int32, full.shape, 1)
    kron[...] = jnp.where(lax.rem(k0, rows) == lax.rem(k1, rows), full, 0.0)

    own[1].wait()
    for m in range(n_lev):
        @pl.when(j != m)
        def _():
            pltpu.make_async_remote_copy(
                thick_s.at[m], thick_r.at[m], thick_ss.at[m], thick_rs.at[m], (i, m), MESH).wait_recv()
    below = jnp.zeros((rows, LANES), jnp.float32)
    for k in reversed(range(n_lev * levels)):
        t = thick_r[k // levels, k % levels]
        dens[k] = jnp.exp((below + 0.5 * t) * (-1.0 / scale_height))
        below = below + t

    own[0].wait()
    zc_copy.wait_recv()

    flow = jnp.zeros((bins, rows, LANES), jnp.float32)
    sub = lax.broadcasted_iota(jnp.int32, (1, rows, LANES), 1)
    lane = lax.broadcasted_iota(jnp.int32, (1, rows, LANES), 2)
    for m in range(n_lev):
        @pl.when(j != m)
        def _():
            pltpu.make_async_remote_copy(
                main_s.at[m], main_r.at[m], main_ss.at[m], main_rs.at[m], (i, m), MESH).wait_recv()

        @pl.when(has_south)
        def _():
            pltpu.make_async_remote_copy(
                north_s.at[m], north_r.at[m], north_ss.at[m], north_rs.at[m], (i - 1, m), MESH).wait_recv()

        @pl.when(has_north)
        def _():
            pltpu.make_async_remote_copy(
                south_s.at[m], south_r.at[m], south_ss.at[m], south_rs.at[m], (i + 1, m), MESH).wait_recv()

        for kk in range(levels):
            k = m * levels + kk
            q = main_r[m, kk, pl.ds(0, bins)]
            mc = main_r[m, kk, pl.ds(bins, 1)]
            t = thick_r[m, pl.ds(kk, 1)]
            q_below = north_r[m, kk, pl.ds(0, bins)][:, None, :]
            q_above = south_r[m, kk, pl.ds(0, bins)][:, None, :]
            mc_above = south_r[m, kk, pl.ds(bins, 1)][:, None, :]
            q_s = jnp.where(sub == 0, q_below, pltpu.roll(q, 1, 1))
            q_n = jnp.where(sub == rows - 1, q_above, pltpu.roll(q, rows - 1, 1))
            mc_n = jnp.where(sub == rows - 1, mc_above, pltpu.roll(mc, rows - 1, 1))
            south = jnp.maximum(mc, 0.0) * q_s + jnp.minimum(mc, 0.0) * q
            north = jnp.maximum(mc_n, 0.0) * q + jnp.minimum(mc_n, 0.0) * q_n
            summed = (q + south - north) + flow
            f = fall_v[...]
            part = summed / (t + f)
            settled = t * part
            flow = f * part
            z = jnp.where(lane == width, pltpu.roll(zc_r[:, k, :][None], width, 2), zc_s[:, k, :][None])
            west = jnp.maximum(z, 0.0) * pltpu.roll(settled, 1, 2) + jnp.minimum(z, 0.0) * settled
            moved = settled + west - pltpu.roll(west, LANES - 1, 2)
            coag = jnp.dot(kron[...], moved.reshape(cells, LANES), precision=HIGHEST,
                           preferred_element_type=jnp.float32).reshape(moved.shape)
            result = moved + dens[pl.ds(k, 1)] * moved * coag
            out_ref[:, :, k, :] = result[:, :, :width]

    below = jnp.zeros((rows, total), jnp.float32)
    for m in range(n_lev):
        @pl.when(j != m)
        def _():
            pltpu.make_async_remote_copy(
                tot_s, tot_r.at[m], tot_ss.at[m], tot_rs.at[m], (i, m), MESH).wait_recv()

        @pl.when(j >= m)
        def _():
            tot_r[m] = jnp.zeros_like(tot_s)
        below = below + tot_r[m][:, :total]
    for k in reversed(range(levels)):
        t = specific_air_factor * temp_ref[:, k, :] * span_ref[k]
        height_ref[:, k, :] = below + 0.5 * t
        below = below + t

    zc_copy.wait_send()
    for m in range(n_lev):
        @pl.when(j != m)
        def _():
            thick_copy(m).wait_send()
            main_copy(m).wait_send()
            tot_copy(m).wait_send()

        @pl.when(has_south)
        def _():
            south_copy(m).wait_send()

        @pl.when(has_north)
        def _():
            north_copy(m).wait_send()


def solution(mesh):
    n_lat, n_lev = mesh.shape["lat"], mesh.shape["lev"]
    vmem = pl.BlockSpec(memory_space=pltpu.VMEM)
    smem = pl.BlockSpec(memory_space=pltpu.SMEM)

    def on_device(q, mc, temp, span, fall, zc, rate):
        bins, rows, levels, total = q.shape
        width = total // n_lev
        assert width + 2 <= LANES
        n_edge = -(-(bins + 1) // 8) * 8
        deep = n_lev * levels
        wide = -(-total // LANES) * LANES
        f32 = jnp.float32
        main = pltpu.VMEM((n_lev, levels, bins + 1, rows, LANES), f32)
        thick = pltpu.VMEM((n_lev, levels, rows, LANES), f32)
        edge = pltpu.VMEM((n_lev, levels, n_edge, LANES), f32)
        zonal = pltpu.VMEM((rows, deep, LANES), f32)
        sems = pltpu.SemaphoreType.DMA((n_lev,))
        pair = pltpu.SemaphoreType.DMA((2,))
        return pl.pallas_call(
            functools.partial(kernel, n_lat, n_lev),
            out_shape=(
                jax.ShapeDtypeStruct((bins, rows, deep, width), f32),
                jax.ShapeDtypeStruct((rows, levels, total), f32),
            ),
            in_specs=[vmem, vmem, vmem, smem, smem, vmem, vmem],
            out_specs=(vmem, vmem),
            scratch_shapes=[
                main, main, thick, thick, edge, edge, edge, edge,
                pltpu.VMEM((rows, wide), f32), pltpu.VMEM((n_lev, rows, wide), f32),
                zonal, zonal,
                pltpu.VMEM((bins, rows, LANES), f32),
                pltpu.VMEM((bins * rows, bins * rows), f32),
                pltpu.VMEM((deep, rows, LANES), f32),
            ] + [sems] * 10 + [pair] * 2,
            compiler_params=pltpu.CompilerParams(
                collective_id=0, has_side_effects=True, vmem_limit_bytes=48 * 1024 * 1024),
        )(q, mc, temp, span, fall, zc, rate)

    in_specs = (
        P(None, "lat", "lev", None),
        P("lat", "lev", None),
        P("lat", "lev", None),
        P("lev"),
        P(),
        P("lat", None, "lev"),
        P(),
    )
    out_specs = (P(None, "lat", None, "lev"), P("lat", "lev", None))
    return jax.shard_map(
        on_device, mesh=mesh, in_specs=in_specs, out_specs=out_specs, check_vma=False
    )
```

time: 57.9 us -> 26.5 us (0.46)
  the two profiles are of different devices: /device:TPU:0 before, /device:TPU:23 now
where the time goes in v1:
time: 26.5 us; the launch traced here: 26.1 us
  Pallas kernels  18.7 us (71%)
  local copies, waits for them, and re-layouts  6.72 us (25%)
  between operations  0.66 us (2%)
    pallas_call x1, Pallas kernels, on_device(): pl.pallas_call(functools.partial(kernel, n_lat, n_lev), out_shape=(jax.Sh...  18.7 us
    unnamed x16, local copies, waits for them, and re-layouts  6.72 us

profile of v1, /device:TPU:23, one launch (start us, length us, event | category | flops | bytes accessed | tf_op | source)
XLA Modules:
  0.0 26.1 jit_solution(9148165127331655317)
XLA Ops:
  0.6 0.0 copy-start
  0.6 1.0 %copy-done = f32[20,8,2,360]{3,2,1,0:T(2,128)S(1)} copy-done((f32[20,8,2,360]{3,2,1,0:T(2,128)S(1)}, f32[20,8,2,360]{3,2,1,0:T(2,128)}, u32[]{:S(2)}) %copy-start) | copy-done | bytes 460824
  1.7 0.0 copy-start.1
  1.7 0.8 %copy-done.1 = f32[8,8,90]{2,1,0:T(8,128)S(1)} copy-done((f32[8,8,90]{2,1,0:T(8,128)S(1)}, f32[8,8,90]{2,1,0:T(8,128)}, u32[]{:S(2)}) %copy-start.1) | copy-done | bytes 23064
  2.4 0.0 copy-start.2
  2.4 0.7 %copy-done.2 = f32[8,2,360]{2,1,0:T(2,128)S(1)} copy-done((f32[8,2,360]{2,1,0:T(2,128)S(1)}, f32[8,2,360]{2,1,0:T(2,128)}, u32[]{:S(2)}) %copy-start.2) | copy-done | bytes 23064
  3.2 0.0 copy-start.3
  3.2 0.7 %copy-done.3 = f32[8,2,360]{2,1,0:T(2,128)S(1)} copy-done((f32[8,2,360]{2,1,0:T(2,128)S(1)}, f32[8,2,360]{2,1,0:T(2,128)}, u32[]{:S(2)}) %copy-start.3) | copy-done | bytes 23064
  3.9 0.0 copy-start.4
  3.9 0.7 %copy-done.4 = f32[20,20]{1,0:T(8,128)S(1)} copy-done((f32[20,20]{1,0:T(8,128)S(1)}, f32[20,20]{1,0:T(8,128)}, u32[]{:S(2)}) %copy-start.4) | copy-done | bytes 1624
  4.6 0.0 copy-start.5
  4.6 0.7 %copy-done.5 = f32[2]{0:T(128)S(1)} copy-done((f32[2]{0:T(128)S(1)}, f32[2]{0:T(128)}, u32[]{:S(2)}) %copy-start.5) | copy-done | bytes 32
  5.3 0.0 copy-start.6
  5.3 0.7 %copy-done.6 = f32[20]{0:T(128)S(1)} copy-done((f32[20]{0:T(128)S(1)}, f32[20]{0:T(128)}, u32[]{:S(2)}) %copy-start.6) | copy-done | bytes 104
  5.9 18.7 %shard_map.86 = (f32[20,8,8,90]{3,2,1,0:T(8,128)S(1)}, f32[8,2,360]{2,1,0:T(2,128)S(1)}) custom-call(f32[20,8,2,360]{3,2,1,0:T(2,128)S(1)} %copy-done, f32[8,2,360]{2,1,0:T(2,128)S(1)} %copy-done.2, f32[8,2,360]{2,1,0:T(2,128)S(1)} %copy-done.3, f32[2]{0:T(128)S(1)} %copy-done.5, f32[20]{0:T(128)S(1)} %copy-done.6, f32[8,8,90]{2,1,0:T(8,128)S(1)} %copy-done.1, ...), custom_call_target="tpu_custom_call" | custom-call | tf_op jit(solution)/shard_map/pallas_call | solution.py:309
  24.7 0.8 %copy.11 = f32[20,8,8,90]{3,2,1,0:T(8,128)} copy(f32[20,8,8,90]{3,2,1,0:T(8,128)S(1)} %get-tuple-element.4) | data formatting | bytes 921600
  25.5 0.6 %copy.12 = f32[8,2,360]{2,1,0:T(2,128)} copy(f32[8,2,360]{2,1,0:T(2,128)S(1)} %get-tuple-element.5) | data formatting | bytes 46080
Async XLA Ops:
  0.6 1.0 %copy-start = (f32[20,8,2,360]{3,2,1,0:T(2,128)S(1)}, f32[20,8,2,360]{3,2,1,0:T(2,128)}, u32[]{:S(2)}) copy-start(f32[20,8,2,360]{3,2,1,0:T(2,128)} %q_ref.1) | copy-start | bytes 1382404
  1.7 0.8 %copy-start.1 = (f32[8,8,90]{2,1,0:T(8,128)S(1)}, f32[8,8,90]{2,1,0:T(8,128)}, u32[]{:S(2)}) copy-start(f32[8,8,90]{2,1,0:T(8,128)} %zc_ref.1) | copy-start | bytes 69124
  2.4 0.7 %copy-start.2 = (f32[8,2,360]{2,1,0:T(2,128)S(1)}, f32[8,2,360]{2,1,0:T(2,128)}, u32[]{:S(2)}) copy-start(f32[8,2,360]{2,1,0:T(2,128)} %mc_ref.1) | copy-start | bytes 69124
  3.2 0.7 %copy-start.3 = (f32[8,2,360]{2,1,0:T(2,128)S(1)}, f32[8,2,360]{2,1,0:T(2,128)}, u32[]{:S(2)}) copy-start(f32[8,2,360]{2,1,0:T(2,128)} %temp_ref.1) | copy-start | bytes 69124
  3.9 0.7 %copy-start.4 = (f32[20,20]{1,0:T(8,128)S(1)}, f32[20,20]{1,0:T(8,128)}, u32[]{:S(2)}) copy-start(f32[20,20]{1,0:T(8,128)} %rate_ref.1) | copy-start | bytes 4804
  4.6 0.7 %copy-start.5 = (f32[2]{0:T(128)S(1)}, f32[2]{0:T(128)}, u32[]{:S(2)}) copy-start(f32[2]{0:T(128)} %span_ref.1) | copy-start | bytes 28
  5.3 0.7 %copy-start.6 = (f32[20]{0:T(128)S(1)}, f32[20]{0:T(128)}, u32[]{:S(2)}) copy-start(f32[20]{0:T(128)} %fall_ref.1) | copy-start | bytes 244

commit v2 on v1

--- a/solution.py
+++ b/solution.py
@@ -46,16 +46,43 @@
     return pltpu.roll(x, (2 * LANES - off - 1) % LANES, axis)
 
 
+def spare(lane, width):
+    return (lane > width) & (lane < LANES - 1)
+
+
+def stow(x, d, width, p):
+    free = LANES - 2 - width
+    lane = lax.broadcasted_iota(jnp.int32, x.shape, 2)
+    return jnp.where(spare(lane, width), pltpu.roll(d, (width + 2 - p * free) % LANES, 2), x)
+
+
+def unstow(parts, width):
+    free = LANES - 2 - width
+    back = [pltpu.roll(x, (p * free - width - 2) % LANES, 2) for p, x in enumerate(parts)]
+    lane = lax.broadcasted_iota(jnp.int32, back[0].shape, 2)
+    later = jnp.where(lane < 2 * free - 1, back[1], back[2])
+    return jnp.where((lane < free - 1) | (lane == LANES - 1), back[0], later)
+
+
 def kernel(
     n_lat, n_lev,
+    q_hbm, mc_hbm, temp_hbm, span_hbm, fall_hbm, zc_hbm, rate_hbm,
+    out_ref, height_ref,
     q_ref, mc_ref, temp_ref, span_ref, fall_ref, zc_ref, rate_ref,
-    out_ref, height_ref,
     main_s, main_r, thick_s, thick_r, north_s, north_r, south_s, south_r,
-    tot_s, tot_r, zc_s, zc_r, fall_v, kron, dens,
+    tot_s, tot_r, zc_s, zc_r, inverse, kron, dens,
     main_ss, main_rs, thick_ss, thick_rs, north_ss, north_rs, south_ss, south_rs,
-    tot_ss, tot_rs, zc_sem, own_sem,
+    tot_ss, tot_rs, zc_sem, own_sem, load_sem,
 ):
     i, j = lax.axis_index("lat"), lax.axis_index("lev")
+    loads = [
+        pltpu.make_async_copy(src, dst, load_sem.at[number])
+        for number, (src, dst) in enumerate((
+            (span_hbm, span_ref), (temp_hbm, temp_ref), (zc_hbm, zc_ref), (mc_hbm, mc_ref),
+            (q_hbm, q_ref), (fall_hbm, fall_ref), (rate_hbm, rate_ref)))
+    ]
+    for load in loads:
+        load.start()
     bins, rows, levels, total = q_ref.shape
     width = total // n_lev
     left, right = lax.rem(j + n_lev - 1, n_lev), lax.rem(j + 1, n_lev)
@@ -75,6 +102,8 @@
         for m in range(n_lev):
             pl.semaphore_signal(barrier, inc=1, device_id=(i + 1, m), device_id_type=MESH)
 
+    for load in loads[:3]:
+        load.wait()
     thick = [specific_air_factor * temp_ref[:, k, :] * span_ref[k] for k in range(levels)]
     tot = thick[0]
     for k in range(1, levels):
@@ -119,8 +148,6 @@
             thick_copy(m).start()
     zc_copy.start()
 
-    last = total - (total // LANES) * LANES
-
     def tile_of(ref, k):
         def tile(c):
             stop = min((c + 1) * LANES, total)
@@ -133,23 +160,25 @@
             return widen(mc_ref[:, k, c * LANES : stop])[None]
         return tile
 
-    for m in range(n_lev):
+    for load in loads[3:5]:
+        load.wait()
+    group = bins // 4
+
+    def send_block(m):
         for k in range(levels):
-            main_s[m, k, pl.ds(0, bins)] = lon_block(tile_of(q_ref, k), total, width, m)
-            main_s[m, k, pl.ds(bins, 1)] = lon_block(mc_tile(k), total, width, m)
+            x = lon_block(tile_of(q_ref, k), total, width, m)
+            for p in range(3):
+                main_s[m, k, pl.ds(p * group, group)] = stow(
+                    x[p * group : (p + 1) * group], x[3 * group :], width, p)
+            main_s[m, k, pl.ds(3 * group, 1)] = lon_block(mc_tile(k), total, width, m)
 
         @pl.when(j != m)
         def _():
             main_copy(m).start()
 
         for k in range(levels):
-            south_s[m, k, pl.ds(0, bins + 1)] = main_s[m, k, :, 0, :]
-            north_s[m, k, pl.ds(0, bins + 1)] = main_s[m, k, :, rows - 1, :]
-        pad = south_s.shape[2] - bins - 1
-        if pad:
-            zero = jnp.zeros((levels, pad, LANES), jnp.float32)
-            south_s[m, :, pl.ds(bins + 1, pad)] = zero
-            north_s[m, :, pl.ds(bins + 1, pad)] = zero
+            south_s[m, k] = main_s[m, k, :, 0, :]
+            north_s[m, k] = main_s[m, k, :, rows - 1, :]
 
         @pl.when(has_south)
         def _():
@@ -159,8 +188,20 @@
         def _():
             north_copy(m).start()
 
-    for m in range(n_lev):
-        @pl.when(j != m)
+    half_way = n_lev // 2
+
+    @pl.when(j >= half_way)
+    def _():
+        for m in range(n_lev):
+            send_block(m)
+
+    @pl.when(j < half_way)
+    def _():
+        for m in range(n_lev):
+            send_block((m + half_way) % n_lev)
+
+    for m in range(n_lev):
+        @pl.when(j > m)
         def _():
             tot_copy(m).start()
 
@@ -177,8 +218,8 @@
     def _():
         south_r[...] = jnp.zeros_like(south_r)
 
-    for b in range(bins):
-        fall_v[b] = jnp.full((rows, LANES), fall_ref[b], jnp.float32)
+    for load in loads[5:]:
+        load.wait()
     rate = rate_ref[...]
     r0 = lax.broadcasted_iota(jnp.int32, rate.shape, 0)
     r1 = lax.broadcasted_iota(jnp.int32, rate.shape, 1)
@@ -205,6 +246,8 @@
         t = thick_r[k // levels, k % levels]
         dens[k] = jnp.exp((below + 0.5 * t) * (-1.0 / scale_height))
         below = below + t
+        for b in range(bins):
+            inverse[k, b] = 1.0 / (t + fall_ref[b])
 
     own[0].wait()
     zc_copy.wait_recv()
@@ -230,22 +273,26 @@
 
         for kk in range(levels):
             k = m * levels + kk
-            q = main_r[m, kk, pl.ds(0, bins)]
-            mc = main_r[m, kk, pl.ds(bins, 1)]
+            q = main_r[m, kk, pl.ds(0, 3 * group)].reshape(3, group, rows, LANES)
+            mc = main_r[m, kk, pl.ds(3 * group, 1)]
             t = thick_r[m, pl.ds(kk, 1)]
-            q_below = north_r[m, kk, pl.ds(0, bins)][:, None, :]
-            q_above = south_r[m, kk, pl.ds(0, bins)][:, None, :]
-            mc_above = south_r[m, kk, pl.ds(bins, 1)][:, None, :]
-            q_s = jnp.where(sub == 0, q_below, pltpu.roll(q, 1, 1))
-            q_n = jnp.where(sub == rows - 1, q_above, pltpu.roll(q, rows - 1, 1))
+            q_below = north_r[m, kk, pl.ds(0, 3 * group)].reshape(3, group, 1, LANES)
+            q_above = south_r[m, kk, pl.ds(0, 3 * group)].reshape(3, group, 1, LANES)
+            mc_above = south_r[m, kk, pl.ds(3 * group, 1)][:, None, :]
             mc_n = jnp.where(sub == rows - 1, mc_above, pltpu.roll(mc, rows - 1, 1))
-            south = jnp.maximum(mc, 0.0) * q_s + jnp.minimum(mc, 0.0) * q
-            north = jnp.maximum(mc_n, 0.0) * q + jnp.minimum(mc_n, 0.0) * q_n
-            summed = (q + south - north) + flow
-            f = fall_v[...]
-            part = summed / (t + f)
-            settled = t * part
-            flow = f * part
+            parts = []
+            for p in range(3):
+                c_s, c_n = stow(mc, mc, width, p), stow(mc_n, mc_n, width, p)
+                x = q[p]
+                q_s = jnp.where(sub == 0, q_below[p], pltpu.roll(x, 1, 1))
+                q_n = jnp.where(sub == rows - 1, q_above[p], pltpu.roll(x, rows - 1, 1))
+                south = jnp.maximum(c_s, 0.0) * q_s + jnp.minimum(c_s, 0.0) * x
+                north = jnp.maximum(c_n, 0.0) * x + jnp.minimum(c_n, 0.0) * q_n
+                parts.append(x + south - north)
+            parts.append(unstow(parts, width))
+            summed = jnp.concatenate(parts, 0) + flow
+            settled = (t * inverse[k]) * summed
+            flow = summed - settled
             z = jnp.where(lane == width, pltpu.roll(zc_r[:, k, :][None], width, 2), zc_s[:, k, :][None])
             west = jnp.maximum(z, 0.0) * pltpu.roll(settled, 1, 2) + jnp.minimum(z, 0.0) * settled
             moved = settled + west - pltpu.roll(west, LANES - 1, 2)
@@ -256,14 +303,15 @@
 
     below = jnp.zeros((rows, total), jnp.float32)
     for m in range(n_lev):
-        @pl.when(j != m)
+        @pl.when(j >= m)
+        def _():
+            tot_r[m] = jnp.zeros_like(tot_s)
+
+        @pl.when(j < m)
         def _():
             pltpu.make_async_remote_copy(
                 tot_s, tot_r.at[m], tot_ss.at[m], tot_rs.at[m], (i, m), MESH).wait_recv()
 
-        @pl.when(j >= m)
-        def _():
-            tot_r[m] = jnp.zeros_like(tot_s)
         below = below + tot_r[m][:, :total]
     for k in reversed(range(levels)):
         t = specific_air_factor * temp_ref[:, k, :] * span_ref[k]
@@ -276,6 +324,9 @@
         def _():
             thick_copy(m).wait_send()
             main_copy(m).wait_send()
+
+        @pl.when(j > m)
+        def _():
             tot_copy(m).wait_send()
 
         @pl.when(has_south)
@@ -290,19 +341,19 @@
 def solution(mesh):
     n_lat, n_lev = mesh.shape["lat"], mesh.shape["lev"]
     vmem = pl.BlockSpec(memory_space=pltpu.VMEM)
-    smem = pl.BlockSpec(memory_space=pltpu.SMEM)
+    hbm = pl.BlockSpec(memory_space=pltpu.HBM)
 
     def on_device(q, mc, temp, span, fall, zc, rate):
         bins, rows, levels, total = q.shape
         width = total // n_lev
-        assert width + 2 <= LANES
-        n_edge = -(-(bins + 1) // 8) * 8
+        assert width + 2 <= 3 * (LANES - 2 - width) and bins % 4 == 0
+        packed = 3 * bins // 4 + 1
         deep = n_lev * levels
         wide = -(-total // LANES) * LANES
         f32 = jnp.float32
-        main = pltpu.VMEM((n_lev, levels, bins + 1, rows, LANES), f32)
+        main = pltpu.VMEM((n_lev, levels, packed, rows, LANES), f32)
         thick = pltpu.VMEM((n_lev, levels, rows, LANES), f32)
-        edge = pltpu.VMEM((n_lev, levels, n_edge, LANES), f32)
+        edge = pltpu.VMEM((n_lev, levels, packed, LANES), f32)
         zonal = pltpu.VMEM((rows, deep, LANES), f32)
         sems = pltpu.SemaphoreType.DMA((n_lev,))
         pair = pltpu.SemaphoreType.DMA((2,))
@@ -312,18 +363,21 @@
                 jax.ShapeDtypeStruct((bins, rows, deep, width), f32),
                 jax.ShapeDtypeStruct((rows, levels, total), f32),
             ),
-            in_specs=[vmem, vmem, vmem, smem, smem, vmem, vmem],
+            in_specs=[hbm] * 7,
             out_specs=(vmem, vmem),
             scratch_shapes=[
+                pltpu.VMEM(q.shape, f32), pltpu.VMEM(mc.shape, f32), pltpu.VMEM(temp.shape, f32),
+                pltpu.SMEM(span.shape, f32), pltpu.SMEM(fall.shape, f32),
+                pltpu.VMEM(zc.shape, f32), pltpu.VMEM(rate.shape, f32),
                 main, main, thick, thick, edge, edge, edge, edge,
                 pltpu.VMEM((rows, wide), f32), pltpu.VMEM((n_lev, rows, wide), f32),
                 zonal, zonal,
-                pltpu.VMEM((bins, rows, LANES), f32),
+                pltpu.VMEM((deep, bins, rows, LANES), f32),
                 pltpu.VMEM((bins * rows, bins * rows), f32),
                 pltpu.VMEM((deep, rows, LANES), f32),
-            ] + [sems] * 10 + [pair] * 2,
+            ] + [sems] * 10 + [pair] * 2 + [pltpu.SemaphoreType.DMA((7,))],
             compiler_params=pltpu.CompilerParams(
-                collective_id=0, has_side_effects=True, vmem_limit_bytes=48 * 1024 * 1024),
+                collective_id=0, has_side_effects=True, vmem_limit_bytes=63 * 1024 * 1024),
         )(q, mc, temp, span, fall, zc, rate)
 
     in_specs = (

time: 26.5 us -> 19.8 us (0.75)
  the two profiles are of different devices: /device:TPU:23 before, /device:TPU:21 now
where the time goes in v2:
time: 19.8 us; the launch traced here: 19.6 us
  Pallas kernels  16.3 us (82%)
  local copies, waits for them, and re-layouts  2.6 us (13%)
  between operations  0.65 us (3%)
    pallas_call x1, Pallas kernels, on_device(): pl.pallas_call(functools.partial(kernel, n_lat, n_lev), out_shape=(jax.Sh...  16.3 us
    unnamed x4, local copies, waits for them, and re-layouts  2.6 us

profile of v2, /device:TPU:21, one launch (start us, length us, event | category | flops | bytes accessed | tf_op | source)
XLA Modules:
  0.0 19.6 jit_solution(3538884830862126339)
XLA Ops:
  0.6 16.3 %shard_map.86 = (f32[20,8,8,90]{3,2,1,0:T(8,128)}, f32[8,2,360]{2,1,0:T(2,128)}) custom-call(f32[20,8,2,360]{3,2,1,0:T(2,128)} %q_hbm.1, f32[8,2,360]{2,1,0:T(2,128)} %mc_hbm.1, f32[8,2,360]{2,1,0:T(2,128)} %temp_hbm.1, f32[2]{0:T(128)} %span_hbm.1, f32[20]{0:T(128)} %fall_hbm.1, f32[8,8,90]{2,1,0:T(8,128)} %zc_hbm.1, f32[20,20]{1,0:T(8,128)} %rate_hbm.1), custom_call_target="tpu_custom_call" | custom-call | tf_op jit(solution)/shard_map/pallas_call | solution.py:360
  17.0 0.0 copy-start
  17.0 2.0 %copy.11 = f32[20,8,8,90]{3,2,1,0:T(8,128)} copy(f32[20,8,8,90]{3,2,1,0:T(8,128)} %get-tuple-element.4) | data formatting | bytes 921600
  19.0 0.0 copy-done
  19.0 0.6 %copy.12 = f32[8,2,360]{2,1,0:T(2,128)} copy(f32[8,2,360]{2,1,0:T(2,128)S(1)} %copy-done) | data formatting | bytes 46080
Async XLA Ops:
  17.0 2.0 %copy-start = (f32[8,2,360]{2,1,0:T(2,128)S(1)}, f32[8,2,360]{2,1,0:T(2,128)}, u32[]{:S(2)}) copy-start(f32[8,2,360]{2,1,0:T(2,128)} %get-tuple-element.5) | copy-start | bytes 69124

commit v3 on v2

--- a/solution.py
+++ b/solution.py
@@ -70,7 +70,7 @@
     out_ref, height_ref,
     q_ref, mc_ref, temp_ref, span_ref, fall_ref, zc_ref, rate_ref,
     main_s, main_r, thick_s, thick_r, north_s, north_r, south_s, south_r,
-    tot_s, tot_r, zc_s, zc_r, inverse, kron, dens,
+    tot_s, tot_r, zc_s, zc_r, inverse, advected, kron, dens,
     main_ss, main_rs, thick_ss, thick_rs, north_ss, north_rs, south_ss, south_rs,
     tot_ss, tot_rs, zc_sem, own_sem, load_sem,
 ):
@@ -117,7 +117,6 @@
     zc_s[...] = widen(zc_ref[...])
 
     peers = n_lev - 1 + n_lev * (jnp.minimum(i, 1) + jnp.minimum(n_lat - 1 - i, 1))
-    pl.semaphore_wait(barrier, peers)
 
     def thick_copy(m):
         return pltpu.make_async_remote_copy(
@@ -141,12 +140,6 @@
 
     zc_copy = pltpu.make_async_remote_copy(
         zc_s, zc_r, zc_sem.at[0], zc_sem.at[1], (i, left), MESH)
-
-    for m in range(n_lev):
-        @pl.when(j != m)
-        def _():
-            thick_copy(m).start()
-    zc_copy.start()
 
     def tile_of(ref, k):
         def tile(c):
@@ -164,22 +157,17 @@
         load.wait()
     group = bins // 4
 
-    def send_block(m):
+    def cut_block(m):
         for k in range(levels):
             x = lon_block(tile_of(q_ref, k), total, width, m)
             for p in range(3):
                 main_s[m, k, pl.ds(p * group, group)] = stow(
                     x[p * group : (p + 1) * group], x[3 * group :], width, p)
             main_s[m, k, pl.ds(3 * group, 1)] = lon_block(mc_tile(k), total, width, m)
-
-        @pl.when(j != m)
-        def _():
-            main_copy(m).start()
-
-        for k in range(levels):
             south_s[m, k] = main_s[m, k, :, 0, :]
             north_s[m, k] = main_s[m, k, :, rows - 1, :]
 
+    def send_edges(m):
         @pl.when(has_south)
         def _():
             south_copy(m).start()
@@ -189,16 +177,47 @@
             north_copy(m).start()
 
     half_way = n_lev // 2
+    base = half_way * (j // half_way)
+
+    def cut_half(first):
+        for m in range(first, first + half_way):
+            cut_block(m)
 
     @pl.when(j >= half_way)
     def _():
-        for m in range(n_lev):
-            send_block(m)
+        cut_half(0)
 
     @pl.when(j < half_way)
     def _():
-        for m in range(n_lev):
-            send_block((m + half_way) % n_lev)
+        cut_half(half_way)
+
+    pl.semaphore_wait(barrier, peers)
+
+    for m in range(n_lev):
+        @pl.when(j != m)
+        def _():
+            thick_copy(m).start()
+    for s in range(half_way):
+        main_copy(half_way - base + s).start()
+    for s in range(half_way):
+        send_edges(half_way - base + s)
+    zc_copy.start()
+
+    @pl.when(j >= half_way)
+    def _():
+        cut_half(half_way)
+
+    @pl.when(j < half_way)
+    def _():
+        cut_half(0)
+
+    for s in range(half_way):
+        m = base + s
+
+        @pl.when(j != m)
+        def _():
+            main_copy(m).start()
+        send_edges(m)
 
     for m in range(n_lev):
         @pl.when(j > m)
@@ -250,12 +269,12 @@
             inverse[k, b] = 1.0 / (t + fall_ref[b])
 
     own[0].wait()
-    zc_copy.wait_recv()
-
-    flow = jnp.zeros((bins, rows, LANES), jnp.float32)
+
     sub = lax.broadcasted_iota(jnp.int32, (1, rows, LANES), 1)
     lane = lax.broadcasted_iota(jnp.int32, (1, rows, LANES), 2)
-    for m in range(n_lev):
+    for s in range(n_lev):
+        m = lax.rem(base + s, n_lev)
+
         @pl.when(j != m)
         def _():
             pltpu.make_async_remote_copy(
@@ -272,10 +291,8 @@
                 south_s.at[m], south_r.at[m], south_ss.at[m], south_rs.at[m], (i + 1, m), MESH).wait_recv()
 
         for kk in range(levels):
-            k = m * levels + kk
             q = main_r[m, kk, pl.ds(0, 3 * group)].reshape(3, group, rows, LANES)
             mc = main_r[m, kk, pl.ds(3 * group, 1)]
-            t = thick_r[m, pl.ds(kk, 1)]
             q_below = north_r[m, kk, pl.ds(0, 3 * group)].reshape(3, group, 1, LANES)
             q_above = south_r[m, kk, pl.ds(0, 3 * group)].reshape(3, group, 1, LANES)
             mc_above = south_r[m, kk, pl.ds(3 * group, 1)][:, None, :]
@@ -290,16 +307,23 @@
                 north = jnp.maximum(c_n, 0.0) * x + jnp.minimum(c_n, 0.0) * q_n
                 parts.append(x + south - north)
             parts.append(unstow(parts, width))
-            summed = jnp.concatenate(parts, 0) + flow
-            settled = (t * inverse[k]) * summed
-            flow = summed - settled
-            z = jnp.where(lane == width, pltpu.roll(zc_r[:, k, :][None], width, 2), zc_s[:, k, :][None])
-            west = jnp.maximum(z, 0.0) * pltpu.roll(settled, 1, 2) + jnp.minimum(z, 0.0) * settled
-            moved = settled + west - pltpu.roll(west, LANES - 1, 2)
-            coag = jnp.dot(kron[...], moved.reshape(cells, LANES), precision=HIGHEST,
-                           preferred_element_type=jnp.float32).reshape(moved.shape)
-            result = moved + dens[pl.ds(k, 1)] * moved * coag
-            out_ref[:, :, k, :] = result[:, :, :width]
+            for p in range(4):
+                advected[m * levels + kk, pl.ds(p * group, group)] = parts[p]
+
+    zc_copy.wait_recv()
+    flow = jnp.zeros((bins, rows, LANES), jnp.float32)
+    for k in range(n_lev * levels):
+        t = thick_r[k // levels, pl.ds(k % levels, 1)]
+        summed = advected[k] + flow
+        settled = (t * inverse[k]) * summed
+        flow = summed - settled
+        z = jnp.where(lane == width, pltpu.roll(zc_r[:, k, :][None], width, 2), zc_s[:, k, :][None])
+        west = jnp.maximum(z, 0.0) * pltpu.roll(settled, 1, 2) + jnp.minimum(z, 0.0) * settled
+        moved = settled + west - pltpu.roll(west, LANES - 1, 2)
+        coag = jnp.dot(kron[...], moved.reshape(cells, LANES), precision=HIGHEST,
+                       preferred_element_type=jnp.float32).reshape(moved.shape)
+        result = moved + dens[pl.ds(k, 1)] * moved * coag
+        out_ref[:, :, k, :] = result[:, :, :width]
 
     below = jnp.zeros((rows, total), jnp.float32)
     for m in range(n_lev):
@@ -373,6 +397,7 @@
                 pltpu.VMEM((rows, wide), f32), pltpu.VMEM((n_lev, rows, wide), f32),
                 zonal, zonal,
                 pltpu.VMEM((deep, bins, rows, LANES), f32),
+                pltpu.VMEM((deep, bins, rows, LANES), f32),
                 pltpu.VMEM((bins * rows, bins * rows), f32),
                 pltpu.VMEM((deep, rows, LANES), f32),
             ] + [sems] * 10 + [pair] * 2 + [pltpu.SemaphoreType.DMA((7,))],

time: 19.8 us -> 18.5 us (0.934)
  the two profiles are of different devices: /device:TPU:21 before, /device:TPU:1 now
where the time goes in v3:
time: 18.5 us; the launch traced here: 18.4 us
  Pallas kernels  15.1 us (82%)
  local copies, waits for them, and re-layouts  2.6 us (14%)
  between operations  0.65 us (4%)
    pallas_call x1, Pallas kernels, on_device(): pl.pallas_call(functools.partial(kernel, n_lat, n_lev), out_shape=(jax.Sh...  15.1 us
    unnamed x4, local copies, waits for them, and re-layouts  2.6 us

profile of v3, /device:TPU:1, one launch (start us, length us, event | category | flops | bytes accessed | tf_op | source)
XLA Modules:
  0.0 18.4 jit_solution(12899928133266044702)
XLA Ops:
  0.6 15.1 %shard_map.86 = (f32[20,8,8,90]{3,2,1,0:T(8,128)}, f32[8,2,360]{2,1,0:T(2,128)}) custom-call(f32[20,8,2,360]{3,2,1,0:T(2,128)} %q_hbm.1, f32[8,2,360]{2,1,0:T(2,128)} %mc_hbm.1, f32[8,2,360]{2,1,0:T(2,128)} %temp_hbm.1, f32[2]{0:T(128)} %span_hbm.1, f32[20]{0:T(128)} %fall_hbm.1, f32[8,8,90]{2,1,0:T(8,128)} %zc_hbm.1, f32[20,20]{1,0:T(8,128)} %rate_hbm.1), custom_call_target="tpu_custom_call" | custom-call | tf_op jit(solution)/shard_map/pallas_call | solution.py:384
  15.8 0.0 copy-start
  15.8 2.0 %copy.11 = f32[20,8,8,90]{3,2,1,0:T(8,128)} copy(f32[20,8,8,90]{3,2,1,0:T(8,128)} %get-tuple-element.4) | data formatting | bytes 921600
  17.8 0.0 copy-done
  17.8 0.6 %copy.12 = f32[8,2,360]{2,1,0:T(2,128)} copy(f32[8,2,360]{2,1,0:T(2,128)S(1)} %copy-done) | data formatting | bytes 46080
Async XLA Ops:
  15.8 2.0 %copy-start = (f32[8,2,360]{2,1,0:T(2,128)S(1)}, f32[8,2,360]{2,1,0:T(2,128)}, u32[]{:S(2)}) copy-start(f32[8,2,360]{2,1,0:T(2,128)} %get-tuple-element.5) | copy-start | bytes 69124

commit v4 on v3

--- a/solution.py
+++ b/solution.py
@@ -362,6 +362,25 @@
             north_copy(m).wait_send()
 
 
+def hand_over(dust_ref, height_ref, dust_out, height_out, dust_v, height_v, sem_in, sem_out):
+    pieces = sem_in.shape[0] - 1
+    step = dust_ref.shape[0] // pieces
+    arrive, leave = [], []
+    for p in range(pieces):
+        part = pl.ds(p * step, step)
+        arrive.append(pltpu.make_async_copy(dust_ref.at[part], dust_v.at[part], sem_in.at[p]))
+        leave.append(pltpu.make_async_copy(dust_v.at[part], dust_out.at[part], sem_out.at[p]))
+    arrive.append(pltpu.make_async_copy(height_ref, height_v, sem_in.at[pieces]))
+    leave.append(pltpu.make_async_copy(height_v, height_out, sem_out.at[pieces]))
+    for copy in arrive:
+        copy.start()
+    for first, second in zip(arrive, leave):
+        first.wait()
+        second.start()
+    for copy in leave:
+        copy.wait()
+
+
 def solution(mesh):
     n_lat, n_lev = mesh.shape["lat"], mesh.shape["lev"]
     vmem = pl.BlockSpec(memory_space=pltpu.VMEM)
@@ -381,7 +400,7 @@
         zonal = pltpu.VMEM((rows, deep, LANES), f32)
         sems = pltpu.SemaphoreType.DMA((n_lev,))
         pair = pltpu.SemaphoreType.DMA((2,))
-        return pl.pallas_call(
+        dust, height = pl.pallas_call(
             functools.partial(kernel, n_lat, n_lev),
             out_shape=(
                 jax.ShapeDtypeStruct((bins, rows, deep, width), f32),
@@ -404,6 +423,17 @@
             compiler_params=pltpu.CompilerParams(
                 collective_id=0, has_side_effects=True, vmem_limit_bytes=63 * 1024 * 1024),
         )(q, mc, temp, span, fall, zc, rate)
+        return pl.pallas_call(
+            hand_over,
+            out_shape=(
+                jax.ShapeDtypeStruct(dust.shape, f32), jax.ShapeDtypeStruct(height.shape, f32)),
+            in_specs=[hbm, hbm],
+            out_specs=(hbm, hbm),
+            scratch_shapes=[
+                pltpu.VMEM(dust.shape, f32), pltpu.VMEM(height.shape, f32),
+                pltpu.SemaphoreType.DMA((5,)), pltpu.SemaphoreType.DMA((5,))],
+            compiler_params=pltpu.CompilerParams(vmem_limit_bytes=63 * 1024 * 1024),
+        )(dust, height)
 
     in_specs = (
         P(None, "lat", "lev", None),

time: 18.5 us -> 17.8 us (0.962)
  local copies, waits for them, and re-layouts: 2.6 us -> 0 us
  Pallas kernels: 15.1 us -> 17 us
    unnamed x4 -> x0, local copies, waits for them, and re-layouts: 2.6 us -> none
    pallas_call x0 -> x1, Pallas kernels: none -> 1.91 us  [on_device(): pl.pallas_call(hand_over, out_shape=(jax.ShapeDtypeStruct(dust.shape, f32...]
where the time goes in v4:
time: 17.8 us; the launch traced here: 17.7 us
  Pallas kernels  17 us (96%)
  between operations  0.64 us (4%)
    pallas_call x1, Pallas kernels, on_device(): pl.pallas_call(functools.partial(kernel, n_lat, n_lev), out_shape=(jax.Sh...  15.1 us
    pallas_call x1, Pallas kernels, on_device(): pl.pallas_call(hand_over, out_shape=(jax.ShapeDtypeStruct(dust.shape, f32...  1.91 us

profile of v4, /device:TPU:1, one launch (start us, length us, event | category | flops | bytes accessed | tf_op | source)
XLA Modules:
  0.0 17.7 jit_solution(6888654511034275267)
XLA Ops:
  0.6 15.1 %shard_map.86 = (f32[20,8,8,90]{3,2,1,0:T(8,128)}, f32[8,2,360]{2,1,0:T(2,128)}) custom-call(f32[20,8,2,360]{3,2,1,0:T(2,128)} %q_hbm.1, f32[8,2,360]{2,1,0:T(2,128)} %mc_hbm.1, f32[8,2,360]{2,1,0:T(2,128)} %temp_hbm.1, f32[2]{0:T(128)} %span_hbm.1, f32[20]{0:T(128)} %fall_hbm.1, f32[8,8,90]{2,1,0:T(8,128)} %zc_hbm.1, f32[20,20]{1,0:T(8,128)} %rate_hbm.1), custom_call_target="tpu_custom_call" | custom-call | tf_op jit(solution)/shard_map/pallas_call | solution.py:403
  15.8 1.9 %shard_map.87 = (f32[20,8,8,90]{3,2,1,0:T(8,128)}, f32[8,2,360]{2,1,0:T(2,128)}) custom-call(f32[20,8,8,90]{3,2,1,0:T(8,128)} %get-tuple-element.4.dust_ref, f32[8,2,360]{2,1,0:T(2,128)} %get-tuple-element.5.height_ref), custom_call_target="tpu_custom_call" | custom-call | tf_op jit(solution)/shard_map/pallas_call | solution.py:426
